TPU v7x, 256 devices: a whole 4x4x8 slice. The times are simulated.
256 devices in a mesh: dp: 256 (over x, y, z, core).
Axes of the slice: x: 4, y: 4, z: 8, core: 2. Of those that a mesh axis runs over, the one named last changes fastest.
Arguments:
- queries: bfloat16 [256, 4096], P('dp'), may hold values from -8 to 8
- passages: bfloat16 [8192, 4096], P('dp'), may hold values from -16 to 16
- positives: int32 [256], replicated, may hold values from 0 to 8160, as said below
- hidden: bfloat16 [256, 256, 4096], P('dp'), may hold values from -6 to 6
- gain_attn: float32 [4096], replicated, may hold values from 0.25 to 1.75
- value_weight: bfloat16 [4096, 1024], replicated, may hold values from -0.09375 to 0.09375
- keys: bfloat16 [256, 256, 1024], P('dp'), may hold values from -6 to 6
- last_query: bfloat16 [256, 4096], P('dp'), may hold values from -160 to 160
- lengths: int32 [256], P('dp'), may hold values from 1 to 256
- gain_final: float32 [4096], replicated, may hold values from 0.25 to 1.75
Outputs:
- mean_loss: float32 [], replicated
- query_grad: float32 [256, 4096], P('dp')
- passage_grad: float32 [8192, 4096], P('dp')
- value_weight_grad: float32 [4096, 1024], P('dp')
- hidden_grad: bfloat16 [256, 256, 4096], P('dp')
Inputs may be any that keep to these rules, and one draw needn't show every extreme that they name: `positives`: each query's positive is the first of some device's 32 passages (its index is a multiple of 32).
All inputs are finite; a program needn't handle non-finite values.
Results may differ from a plain program's by a relative error of at most 0.012.
Values may be sent and summed in bfloat16 or wider, within the bound.
A program may use at most 128 MiB of HBM per device.

v0:
```python
import math

import jax
import jax.numpy as jnp
from jax import lax
from jax.sharding import PartitionSpec as P

HEADS = 32
KV_HEADS = 8
HEAD_DIM = 128


def unit_rows(matrix):
    divisor = jnp.sqrt(jnp.sum(matrix * matrix, axis=1) + 1e-06)
    return (matrix / divisor[:, None], divisor)


def tangent(gradient, unit, divisor):
    return (gradient - unit * jnp.sum(unit * gradient, axis=1, keepdims=True)) / divisor[:, None]


def window(hidden, gain_attn, value_weight, keys, last_query, lengths, demb, gain_final):
    count, seq_len, width = hidden.shape
    kv_width = value_weight.shape[1]
    groups = HEADS // KV_HEADS
    hidden_wide = hidden.astype(jnp.float32)
    rscale = lax.rsqrt(jnp.mean(hidden_wide * hidden_wide, axis=-1) + 1e-05)
    normed = (hidden_wide * rscale[..., None] * gain_attn).astype(jnp.bfloat16)
    flat_normed = normed.reshape(count * seq_len, width)
    values = jnp.dot(flat_normed, value_weight, preferred_element_type=jnp.float32).astype(
        jnp.bfloat16
    )
    query_heads = last_query.astype(jnp.float32).reshape(count, KV_HEADS, groups, HEAD_DIM)
    key_heads = keys.astype(jnp.float32).reshape(count, seq_len, KV_HEADS, HEAD_DIM)
    logits = jnp.einsum("bkgd,btkd->bkgt", query_heads, key_heads) / math.sqrt(HEAD_DIM)
    positions = jnp.arange(seq_len, dtype=jnp.int32)
    visible = positions[None, :] < lengths[:, None]
    logits = jnp.where(visible[:, None, None, :], logits, -1e30)
    row_peak = jnp.max(logits, axis=-1, keepdims=True)
    weights = jnp.exp(logits - row_peak)
    weights = weights / jnp.sum(weights, axis=-1, keepdims=True)
    value_heads = values.astype(jnp.float32).reshape(count, seq_len, KV_HEADS, HEAD_DIM)
    context = jnp.einsum("bkgt,btkd->bkgd", weights, value_heads).reshape(count, width)
    last_pick = (positions[None, :] == lengths[:, None] - 1).astype(jnp.float32)
    final_in = jnp.einsum("bt,btd->bd", last_pick, hidden_wide)
    final_state = final_in + context
    oscale = lax.rsqrt(jnp.mean(final_state * final_state, axis=-1) + 1e-05)
    upstream = demb * gain_final
    dstate = oscale[:, None] * (
        upstream
        - final_state
        * (oscale**2)[:, None]
        * jnp.mean(upstream * final_state, axis=-1, keepdims=True)
    )
    dcontext = dstate.reshape(count, KV_HEADS, groups, HEAD_DIM)
    dvalues_full = jnp.einsum("bkgt,bkgd->btkd", weights, dcontext).reshape(
        count * seq_len, kv_width
    )
    dvalues = dvalues_full.astype(jnp.bfloat16)
    dnormed = jnp.dot(dvalues, value_weight.T, preferred_element_type=jnp.float32).reshape(
        count, seq_len, width
    )
    inner_grad = dnormed * gain_attn
    input_grad = rscale[..., None] * (
        inner_grad
        - hidden_wide
        * (rscale**2)[..., None]
        * jnp.mean(inner_grad * hidden_wide, axis=-1, keepdims=True)
    )
    input_grad = input_grad + last_pick[..., None] * dstate[:, None, :]
    return (input_grad.astype(jnp.bfloat16), flat_normed, dvalues_full, weights, dstate)


def per_device(
    queries,
    passages,
    positives,
    hidden,
    gain_attn,
    value_weight,
    keys,
    last_query,
    lengths,
    gain_final,
):
    precise = lax.Precision.HIGHEST
    every_query = lax.all_gather(queries, "dp", axis=0, tiled=True)
    q_unit, q_norm = unit_rows(every_query.astype(jnp.float32))
    p_unit, p_norm = unit_rows(passages.astype(jnp.float32))
    scores = 50.0 * jnp.dot(q_unit, p_unit.T, precision=precise)
    expo_terms = jnp.exp(scores - 50.0)
    local_count = passages.shape[0]
    first_column = lax.axis_index("dp") * local_count
    column = first_column + jnp.arange(local_count, dtype=jnp.int32)
    target = (positives[:, None] == column[None, :]).astype(jnp.float32)
    totals, positive_hits = lax.psum(
        (jnp.sum(expo_terms, axis=1), jnp.sum(target * scores, axis=1)), "dp"
    )
    mean_loss = jnp.mean(jnp.log(totals) + 50.0 - positive_hits)
    coefficient = 50.0 * (expo_terms / totals[:, None] - target)
    own_rows = queries.shape[0]
    own_first = lax.axis_index("dp") * own_rows
    block = coefficient
    query_sum = lax.psum_scatter(
        jnp.dot(block, p_unit, precision=precise), "dp", scatter_dimension=0, tiled=True
    )
    own_unit = lax.dynamic_slice_in_dim(q_unit, own_first, own_rows, 0)
    own_norm = lax.dynamic_slice_in_dim(q_norm, own_first, own_rows, 0)
    query_grad = tangent(query_sum, own_unit, own_norm)
    passage_sum = jnp.dot(coefficient.T, q_unit, precision=precise)
    passage_grad = tangent(passage_sum, p_unit, p_norm)
    window_count, seq_len, width = hidden.shape
    hidden_grad, flat_normed, dvalues_full, weights, dstate = window(
        hidden,
        gain_attn,
        value_weight,
        keys,
        last_query,
        lengths,
        passage_grad[:window_count],
        gain_final,
    )
    block = flat_normed.astype(jnp.float32)
    value_weight_grad = lax.psum_scatter(
        lax.dot_general(
            block,
            dvalues_full,
            (((0,), (0,)), ((), ())),
            precision=precise,
            preferred_element_type=jnp.float32,
        ),
        "dp",
        scatter_dimension=0,
        tiled=True,
    )
    return (mean_loss, query_grad, passage_grad, value_weight_grad, hidden_grad)


def solution(mesh):
    placed = (
        P("dp", None),
        P("dp", None),
        P(),
        P("dp", None, None),
        P(),
        P(),
        P("dp", None, None),
        P("dp", None),
        P("dp"),
        P(),
    )
    return jax.shard_map(
        per_device,
        mesh=mesh,
        in_specs=placed,
        out_specs=(P(), P("dp", None), P("dp", None), P("dp", None), P("dp", None, None)),
        check_vma=False,
    )
```

profile of v0, /device:TPU:1, one launch (start us, length us, event | category | flops | bytes accessed | tf_op | source)
XLA Modules:
  0.0 1797.4 jit_solution(13808950367701927445)
XLA Ops:
  7.2 0.0 copy-start
  7.2 0.0 all-gather.3.cloned.1.call-start
  7.2 0.7 all-gather.3.cloned.1.call-update
  7.9 0.0 all-reduce.4.cloned.1.call-start
  8.6 1.1 copy.21
  9.8 0.0 copy-done
  9.8 0.1 reduce.10
  9.8 0.3 fusion.43
  10.1 0.2 fusion.30
  10.3 2.1 fusion.1
  12.4 0.0 copy-start.2
  12.4 0.0 copy-start.3
  12.4 6.6 fusion.14
  19.0 0.2 fusion.20
  19.3 0.0 copy-done.2
  19.3 0.4 fusion.12
  19.6 0.6 multiply_reduce_fusion.2
  21.0 0.0 copy-done.3
  21.0 0.2 fusion.19
  21.2 110.0 %all-gather.3.cloned.1.call-done = bf16[256,1,4096]{2,1,0:T(2,128)(2,1)} async-done(((bf16[1,1,4096]{2,1,0:T(2,128)(2,1)}), bf16[256,1,4096]{2,1,0:T(2,128)(2,1)}) %all-gather.3.cloned.1.call-update) | async-done | bytes 2097168 | tf_op jit(solution)/shard_map/all_gather | solution.py:87
  131.2 6.5 convert_element_type.46
  137.7 2.2 fusion.10
  139.9 0.0 copy-start.6
  139.9 4.2 bitcast_divide_fusion
  144.2 0.0 copy-start.1
  144.2 1.9 copy-done.1
  146.1 0.0 copy-done.6
  146.1 3.8 fusion.28
  149.9 74.8 %all-reduce.1 = (f32[256]{0:T(256)S(1)}, f32[256]{0:T(256)S(1)}) all-reduce(f32[256]{0:T(256)S(1)} %get-tuple-element.6, f32[256]{0:T(256)S(1)} %get-tuple-element.5), channel_id=1, replica_groups=mesh['dp'=256] {'dp'}, use_global_device_ids=true, to_apply=%region_5.0 | all-reduce | flops 512 | bytes 4096 | tf_op jit(solution)/shard_map/psum | solution.py:96
  224.6 5.2 fusion.38
  229.8 0.0 copy-start.5
  229.8 4.8 multiply_reduce_fusion
  234.6 0.0 copy-start.4
  234.6 0.0 all-reduce.4.cloned.1.call-update
  234.6 0.3 reduce-scatter.2.cloned.1.call-start
  234.9 1.0 subtract_divide_fusion
  235.9 0.0 copy-done.5
  235.9 1.5 multiply_reduce_fusion.1
  238.1 0.9 subtract_multiply_fusion
  239.0 1.3 fusion.40
  240.4 0.0 copy-done.4
  240.4 13.1 fusion.16
  253.4 0.0 reduce-scatter.2.cloned.1.call-update
  253.5 0.7 dynamic_slice.7
  254.1 0.6 subtract_reduce_fusion
  255.4 6.6 fusion.9
  262.1 3.1 fusion.8
  265.1 232.2 %all-reduce.4.cloned.1.call-done = f32[256,4096]{1,0:T(8,128)} async-done(((f32[256,4096]{1,0:T(8,128)}), f32[256,4096]{1,0:T(8,128)}) %all-reduce.4.cloned.1.call-update) | async-done | bytes 4194320
  497.3 1.6 multiply_reduce_fusion.3
  498.9 2.9 subtract_divide_fusion.1
  501.8 1287.9 %reduce-scatter.2.cloned.1.call-done = f32[16,1024]{1,0:T(8,128)} async-done(((f32[4096,1024]{1,0:T(8,128)}), f32[16,1024]{1,0:T(8,128)}) %reduce-scatter.2.cloned.1.call-update) | async-done | bytes 65552 | tf_op jit(solution)/shard_map/reduce_scatter | solution.py:124
  (8 shorter events, 0.1 us)
Async XLA Ops:
  7.2 2.6 copy-start
  7.2 124.0 %all-gather.3.cloned.1.call-start = ((), (), s32[]{:S(2)}) async-start(), calls=%async_computation.2 | async-start | bytes 4210688 | tf_op jit(solution)/shard_map/all_gather | solution.py:87
  7.9 489.4 %all-reduce.4.cloned.1.call-start = ((), (), s32[]{:S(2)}) async-start(), calls=%async_computation.3 | async-start | bytes 8388608
  12.4 6.8 copy-start.2
  12.4 8.5 copy-start.3
  139.9 6.2 copy-start.6
  144.2 1.9 copy-start.1
  229.8 6.1 copy-start.5
  234.6 5.8 copy-start.4
  234.6 1555.1 %reduce-scatter.2.cloned.1.call-start = ((), (), s32[]{:S(2)}) async-start(), calls=%async_computation.1 | async-start | bytes 16842752 | tf_op jit(solution)/shard_map/reduce_scatter | solution.py:124
Sparse Core Ops, SparseCore 0:
  11.7 119.3 all-gather.2
  234.8 262.4 all-reduce.3
  500.5 1289.1 reduce-scatter.1
where the time goes:
time: 1800 us
  waiting for transfers between devices  1630 us (91%)
  blocking collectives  74.8 us (4%)
  matrix products  42.3 us (2%)
  other arithmetic  27.7 us (2%)
    reduce_scatter x1, waiting for transfers between devices, per_device(): lax.psum_scatter(lax.dot_general(block, dvalues_full, (((0,), (0,)), ((),...  1290 us
    unnamed x4, waiting for transfers between devices  233 us
    all_gather x1, waiting for transfers between devices, per_device(): every_query = lax.all_gather(queries, 'dp', axis=0, tiled=True)  110 us
    psum x1, blocking collectives, per_device(): lax.psum((jnp.sum(expo_terms, axis=1), jnp.sum(target * scores, axis=1)),...  74.8 us
  transfers between devices with their start and end apart: 3, of which 3 were waited for; matrix products, arithmetic and copies ran while one was open for 3% of the time, Pallas kernels for 0%

commit v1 on v0

v1 whole, which is shorter than its diff:
```python
import math

import jax
import jax.numpy as jnp
from jax import lax
from jax.experimental import pallas as pl
from jax.experimental.pallas import tpu as pltpu
from jax.sharding import PartitionSpec as P

HEADS = 32
KV_HEADS = 8
HEAD_DIM = 128
D = 4096
HALF = 2048
QCOL = 1024
BCOL = QCOL + 128
SEQ = 256
KVW = 1024
F32 = jnp.float32
BF16 = jnp.bfloat16
MESH = pl.DeviceIdType.MESH


def dot(a, b, ca, cb):
    return lax.dot_general(a, b, (((ca,), (cb,)), ((), ())), preferred_element_type=F32)


def total(v):
    return jnp.sum(jnp.sum(v, axis=1, keepdims=True), axis=0, keepdims=True)


def kernel(
    lengths, queries, passages, positives, hidden, gain_attn, value_weight, keys, last_query, gain_final,
    loss_out, query_out, passage_out, weight_out, hidden_out,
    len_in, q_in, p_all, pos_in, h_in, ga_in, wv_in, k_in, lq_in, gf_in,
    perm, rows32, q_rows, q_half, q_recv, q_a, q_b, s_own, s_all,
    tot_own, tot_a, tot_b, pool_own, pool_recv, pool_t, pool_rows, lhs_all, rhs_all, w_send, w_recv,
    wts, hcol, pg, spread, drow, hg, pool_rows32, wts_t,
    v1, va1, vb1, v_fwd, v2a, v2b, va2, vb2, v3, v3_recv, wg, qg,
    in_sem, out_sem, grp_send, grp_recv, one_send, one_recv, loc_sem,
):
    me = lax.axis_index("dp")
    g, i = me // 16, me % 16
    x, y, core = g // 4, g % 4, i % 2
    other = 1 - core
    sibling = g * 16 + (i + 1 - 2 * core)

    def grp_dev(j):
        return g * 16 + lax.rem(i + j, 16)

    def z_dev(j):
        return g * 16 + lax.rem(i + 2 * j, 16)

    def xy_dev(j):
        return lax.rem(g + j, 16) * 16 + i

    def x_dev(j):
        return (lax.rem(x + j, 4) * 4 + y) * 16 + i

    def y_dev(j):
        return (x * 4 + lax.rem(y + j, 4)) * 16 + i

    loads = []
    for n, (src, dst) in enumerate(
        (
            (queries, q_in), (lengths, len_in), (last_query, lq_in), (keys, k_in), (passages, p_all.at[core]), (hidden, h_in),
            (value_weight, wv_in), (positives, pos_in), (gain_attn, ga_in), (gain_final, gf_in),
        )
    ):
        copy = pltpu.make_async_copy(src, dst, in_sem.at[n])
        copy.start()
        loads.append(copy)
    l_query, l_len, l_last, l_keys, l_pass, l_hidden, l_value, l_pos, l_ga, l_gf = loads

    barrier = pltpu.get_barrier_semaphore()

    def greet(j, _):
        pl.semaphore_signal(barrier, inc=1, device_id=(grp_dev(j),), device_id_type=MESH)
        pl.semaphore_signal(barrier, inc=1, device_id=(xy_dev(j),), device_id_type=MESH)
        return 0

    lax.fori_loop(1, 16, greet, 0, unroll=True)

    def x_far(j):
        return x_dev(j) + 1 - 2 * core

    for j in range(1, 4):
        pl.semaphore_signal(barrier, inc=1, device_id=(x_far(j),), device_id_type=MESH)

    sends = []

    def send(src, dst, n, dev):
        copy = pltpu.make_async_remote_copy(
            src_ref=src, dst_ref=dst, send_sem=one_send.at[n], recv_sem=one_recv.at[n],
            device_id=(dev,), device_id_type=MESH,
        )
        copy.start()
        sends.append(copy)

    def arrived(ref, n):
        pltpu.make_async_remote_copy(
            src_ref=ref, dst_ref=ref, send_sem=one_send.at[n], recv_sem=one_recv.at[n],
            device_id=(sibling,), device_id_type=MESH,
        ).wait_recv()

    sprays = []

    def spray(n, device, src_of, dst_of, whole, stop=16):
        def step(j, _):
            pltpu.make_async_remote_copy(
                src_ref=src_of(j), dst_ref=dst_of(j), send_sem=grp_send.at[n], recv_sem=grp_recv.at[n],
                device_id=(device(j),), device_id_type=MESH,
            ).start()
            return 0

        lax.fori_loop(1, stop, step, 0, unroll=True)
        pltpu.make_async_copy(src_of(0), dst_of(0), grp_recv.at[n]).start()
        some = whole.at[pl.ds(0, stop - 1)]
        sprays.append(pltpu.make_async_copy(some, some, grp_send.at[n]))
        return pltpu.make_async_copy(whole, whole, grp_recv.at[n])

    l_query.wait()
    for r in range(32):
        q_rows[r : r + 1, :] = q_in[0:1, r * 128 : (r + 1) * 128].astype(F32)
    q_half[0] = q_rows[0:16, :].astype(BF16)
    q_half[1] = q_rows[16:32, :].astype(BF16)
    row = lax.broadcasted_iota(jnp.int32, (256, 256), 0)
    col = lax.broadcasted_iota(jnp.int32, (256, 256), 1)
    swap = ((row >> 4) == (col & 15)) & ((row & 15) == (col >> 4))
    perm[...] = jnp.where(swap, 1.0, 0.0).astype(BF16)

    pl.semaphore_wait(barrier, 33)

    q_came = spray(0, grp_dev, lambda j: q_half.at[lax.rem(i + j, 2)], lambda j: q_recv.at[i], q_recv)

    l_pass.wait()
    send(p_all.at[core], p_all.at[core], 52, sibling)

    l_last.wait()
    for r in range(32):
        rows32[r : r + 1, :] = lq_in[0:1, r * 128 : (r + 1) * 128].astype(F32)
    head = lax.broadcasted_iota(jnp.int32, (HEADS, KVW), 0) >> 2
    kv = lax.broadcasted_iota(jnp.int32, (HEADS, KVW), 1) >> 7
    same_kv = head == kv
    lq = rows32[...]
    query_wide = jnp.where(same_kv, jnp.concatenate([lq] * KV_HEADS, axis=1), 0.0).astype(BF16)
    l_keys.wait()
    logits = dot(query_wide, k_in[...], 1, 1) * (1.0 / math.sqrt(HEAD_DIM))
    token = lax.broadcasted_iota(jnp.int32, (HEADS, SEQ), 1)
    l_len.wait()
    count = len_in[0]
    logits = jnp.where(token < count, logits, -1e30)
    weights = jnp.exp(logits - jnp.max(logits, axis=1, keepdims=True))
    weights = weights / jnp.sum(weights, axis=1, keepdims=True)
    pick = jnp.where(lax.broadcasted_iota(jnp.int32, (16, SEQ), 1) == count - 1, 1.0, 0.0)
    pick = jnp.where(lax.broadcasted_iota(jnp.int32, (16, SEQ), 0) == 0, pick, 0.0)

    q_came.wait()
    turned = dot(perm[...], q_recv[...].reshape(256, 128), 1, 0)
    square = jnp.zeros((16, 128), F32)
    for j in range(16):
        part = turned[j * 16 : (j + 1) * 16, :]
        square = square + part * part
        part = part.astype(BF16)
        if j < 8:
            q_a[core, x, y, :, j * 128 : (j + 1) * 128] = part
        else:
            q_b[core, x, y, :, (j - 8) * 128 : (j - 7) * 128] = part
    square = jnp.broadcast_to(jnp.sum(square, axis=1, keepdims=True), (16, 128))
    top = square.astype(BF16)
    mid = (square - top.astype(F32)).astype(BF16)
    low = square - top.astype(F32) - mid.astype(F32)
    lane = lax.broadcasted_iota(jnp.int32, (16, 128), 1)
    ext = jnp.where(lane == 0, top.astype(F32), jnp.where(lane == 1, mid.astype(F32), jnp.where(lane == 2, low, 0.0)))
    q_b[core, x, y, :, QCOL:BCOL] = ext.astype(BF16)

    low, high, every = pl.ds(0, 2), pl.ds(2, 2), slice(None)

    def rest_of(order, h, near, part=every):
        return q_a.at[h, near, part] if order == 0 else q_b.at[h, part, near]

    def here(order):
        return x if order == 0 else y

    def along(order, j):
        return x_dev(j) if order == 0 else y_dev(j)

    def pass_ref(ref, n, dev):
        send(ref, ref, n, dev)

    def q_block():
        for j in range(1, 4):
            pass_ref(q_a.at[core, x, y], j, y_dev(j))
            pass_ref(q_b.at[core, x, y], 4 + j, x_dev(j))

    def q_line():
        for j in range(1, 4):
            arrived(q_a.at[core, x, lax.rem(y + 4 - j, 4)], j)
            arrived(q_b.at[core, lax.rem(x + 4 - j, 4), y], 4 + j)
        for order in range(2):
            line = rest_of(order, core, here(order))
            pass_ref(line, 9 + 4 * order, along(order, 1))
            pass_ref(line, 11 + 4 * order, along(order, 3))
        for order in range(2):
            pass_ref(rest_of(order, core, here(order)), 16 + 4 * order, sibling)

    def q_pass():
        for side, part in ((1, low), (3, high)):
            for order in range(2):
                near = lax.rem(here(order) + 4 - side, 4)
                arrived(rest_of(order, core, near), 8 + 4 * order + side)
                pass_ref(rest_of(order, core, near, part), 8 + 4 * order + (2 if side == 1 else 0), along(order, side))
                pass_ref(rest_of(order, core, near), 16 + 4 * order + side, sibling)
        for side, part in ((1, low), (3, high)):
            for order in range(2):
                far = lax.rem(here(order) + 2, 4)
                arrived(rest_of(order, core, far, part), 8 + 4 * order + (2 if side == 1 else 0))
                pass_ref(rest_of(order, core, far, part), 18 + 4 * order if side == 1 else 40 + order, sibling)

    def q_finish():
        for order in range(2):
            for side in (0, 1, 3):
                arrived(rest_of(order, other, lax.rem(here(order) + 4 - side, 4)), 16 + 4 * order + side)
            far = lax.rem(here(order) + 2, 4)
            arrived(rest_of(order, other, far, low), 18 + 4 * order)
            arrived(rest_of(order, other, far, high), 40 + order)

    def q_block_of(h, order):
        return (q_b if order else q_a)[h, :, :, :, 0:QCOL].reshape(256, QCOL)

    q_block()

    l_hidden.wait()

    def norm_rows(b, _):
        rows = pl.ds(pl.multiple_of(b * 16, 16), 16)
        part = h_in[rows, :].astype(F32)
        hcol[rows, :] = jnp.broadcast_to(jnp.sum(part * part, axis=1, keepdims=True), (16, 128))
        return 0

    lax.fori_loop(0, 16, norm_rows, 0, unroll=True)
    rs_col = lax.rsqrt(hcol[...] * (1.0 / D) + 1e-05)
    rs_row = jnp.transpose(rs_col)[0:1, :]
    scaled = weights * rs_row
    wts[0:32, :] = scaled.astype(BF16)
    wts[32:48, :] = pick.astype(BF16)
    wts_t[...] = jnp.transpose(jnp.concatenate([scaled, pick, jnp.zeros((80, SEQ), F32)], axis=0))[:, 0:48].astype(BF16)

    q_line()

    l_ga.wait()
    for n in range(8):
        cols = slice(n * 512, (n + 1) * 512)
        both = dot(wts[...], h_in[:, cols], 1, 0)
        drow[:, cols] = both[32:48, :]
        pooled = (both[0:32, :] * ga_in[:, cols]).astype(BF16)
        pool_rows32[:, cols] = pooled
        for p in (2 * n, 2 * n + 1):
            piece = pooled[:, (p - 2 * n) * 256 : (p - 2 * n + 1) * 256]
            spot = slice((p // 4) * 256, (p // 4 + 1) * 256)
            pool_own[p % 4, 0, :, spot] = piece[0:16, :]
            pool_own[p % 4, 1, :, spot] = piece[16:32, :]
    l_value.wait()

    def context(n):
        cols = slice(n * 512, (n + 1) * 512)
        wide = jnp.where(same_kv[:, cols], dot(pool_rows32[...], wv_in[:, cols], 1, 0), 0.0)
        return (wide[:, 0:128] + wide[:, 128:256]) + (wide[:, 256:384] + wide[:, 384:512])

    final = context(0)

    arrived(p_all.at[other], 52)
    wide_p = p_all[...].reshape(64, D).astype(F32)
    p_norm = jnp.sqrt(jnp.sum(wide_p * wide_p, axis=1, keepdims=True) + 1e-06)

    q_pass()

    for j in range(1, 4):
        send(pool_own.at[lax.rem(y + j, 4)], pool_recv.at[y], 24 + j, y_dev(j))
    keep_pool = pltpu.make_async_copy(pool_own.at[y], pool_recv.at[y], one_recv.at[24])
    keep_pool.start()

    rhs_all[...] = jnp.zeros((2048, 256), BF16)

    q_finish()
    l_pos.wait()
    three = jnp.where(lax.broadcasted_iota(jnp.int32, (16, 128), 1) < 3, 1.0, 0.0).astype(BF16)
    dots = jnp.zeros((64, 256), F32)
    q_square = jnp.zeros((16, 256), F32)
    for h in range(2):
        for order in range(2):
            first = h * HALF + order * QCOL
            dots = dots + dot(
                p_all[:, :, first : first + QCOL].reshape(64, QCOL), q_block_of(h, order), 1, 1
            )
        q_square = q_square + dot(three, q_b[h, :, :, :, QCOL:BCOL].reshape(256, 128), 1, 1)
    q_norm = jnp.sqrt(q_square[0:1, :] + 1e-06)
    cosine = dots / (p_norm * q_norm)
    scores = 50.0 * cosine
    expo = jnp.exp(scores - 50.0)
    column = (me - core) * 32 + lax.broadcasted_iota(jnp.int32, (64, 256), 0)
    target = jnp.where(pos_in[...] == column, 1.0, 0.0)
    tot_own[0, :, 0:256] = jnp.sum(expo, axis=0, keepdims=True)
    tot_own[0, :, 256:512] = jnp.sum(target * scores, axis=0, keepdims=True)
    tot_came = spray(3, z_dev, lambda j: tot_own.at[0], lambda j: tot_a.at[i // 2], tot_a, 8)

    keep_pool.wait()
    for j in range(1, 4):
        arrived(pool_recv.at[lax.rem(y + 4 - j, 4)], 24 + j)
    for h in range(2):
        half_rows = [pool_recv[:, h, :, xp * 512 : (xp + 1) * 512].reshape(64, 512).astype(F32) for xp in range(2)]
        turned = jnp.transpose(jnp.concatenate(half_rows, axis=0)).astype(BF16)
        for xl in range(2):
            pool_t[h, :, xl] = turned[xl * 256 : (xl + 1) * 256, :].reshape(8, 32, 128)
    rows_came = spray(
        2, grp_dev,
        lambda j: pool_t.at[lax.rem(i + j, 2), lax.rem(i + j, 16) // 2], lambda j: pool_rows.at[i], pool_rows,
    )

    tot_came.wait()
    acc = tot_a[0]
    for s in range(1, 8):
        acc = acc + tot_a[s]
    tot_own[1] = acc
    tot_came = spray(4, xy_dev, lambda j: tot_own.at[1], lambda j: tot_b.at[g], tot_b)

    final = final + context(1)
    for r in range(32):
        rows32[r : r + 1, :] = drow[0:1, r * 128 : (r + 1) * 128]
    final = final + rows32[...]
    oscale = lax.rsqrt(total(final * final) * (1.0 / D) + 1e-05)
    inv_p = 1.0 / p_norm
    tot_came.wait()
    acc = tot_b[0]
    for s in range(1, 16):
        acc = acc + tot_b[s]
    totals = acc[:, 0:256]
    coeff = 50.0 * (expo / totals - target)

    def v1_part(order, j, part):
        to = lax.rem(here(order) + j, 4)
        return v1.at[0, to, part] if order == 0 else v1.at[1, part, to]

    def ring(order, side, n):
        return (vb1 if order else va1).at[n + (0 if side == 1 else 3)]

    def ring_sem(order, side, n):
        return (49 if side == 1 else 42) + n + (4 if order and side == 1 else 3 if order else 0)

    by_p = jnp.transpose(jnp.concatenate([coeff * inv_p, jnp.zeros((64, 256), F32)], axis=0))[:, 0:64].astype(BF16)
    for order in range(2):
        for n in range(2):
            cols = pl.ds(pl.multiple_of(core * HALF + (order * QCOL + n * 512), 512), 512)
            part = dot(by_p, p_all[:, :, cols].reshape(64, 512), 1, 0)
            v1[order, :, :, :, n * 512 : (n + 1) * 512] = part.astype(BF16).reshape(4, 4, 16, 512)
        for side, part, rest in ((1, low, high), (3, high, low)):
            send(v1_part(order, 2, part), ring(order, side, 0), ring_sem(order, side, 0), along(order, side))
            send(v1_part(order, side, rest), ring(order, side, 1), ring_sem(order, side, 1), along(order, side))

    def own_rows(rows):
        return jnp.where(core == 0, rows[0:32], rows[32:64])

    by_q = (own_rows(coeff) / q_norm).astype(BF16)
    radial = own_rows(jnp.sum(coeff * cosine, axis=1, keepdims=True) * inv_p)
    inv_own = own_rows(inv_p)
    for n in range(4):
        cols = slice(n * QCOL, (n + 1) * QCOL)
        p_sum = dot(by_q, q_block_of(n // 2, n % 2), 1, 0)
        pg[:, cols] = (p_sum - p_all[core, :, cols].astype(F32) * radial) * inv_own
    out_p = pltpu.make_async_copy(pg, passage_out, out_sem.at[0])
    out_p.start()

    for r in range(32):
        rows32[r : r + 1, :] = pg[0:1, r * 128 : (r + 1) * 128]
    l_gf.wait()
    upstream = rows32[...] * gf_in[...]
    mean_uf = total(upstream * final) * (1.0 / D)
    dstate = oscale * (upstream - final * (oscale * oscale) * mean_uf)
    s_own[0] = dstate[0:16, :].astype(BF16)
    s_own[1] = dstate[16:32, :].astype(BF16)
    s_came = spray(5, grp_dev, lambda j: s_own.at[lax.rem(i + j, 2)], lambda j: s_all.at[y, i], s_all.at[y])

    for order in range(2):
        for side, part in ((1, low), (3, high)):
            arrived(ring(order, side, 0), ring_sem(order, side, 0))
            added = v1_part(order, side, part)[...].astype(F32) + ring(order, side, 0)[...].astype(F32)
            slot = order * 2 + (0 if side == 1 else 1)
            v_fwd[slot] = added.astype(BF16)
            send(v_fwd.at[slot], ring(order, side, 2), ring_sem(order, side, 2), along(order, side))

    rows_came.wait()
    lane_kv = (lax.broadcasted_iota(jnp.int32, (64, 128), 1) & 15) >> 2
    for s in range(16):
        rows = pool_rows[s].reshape(64, 128).astype(F32)
        for k in range(4):
            lhs_all[k * 64 : (k + 1) * 64, s * 128 : (s + 1) * 128] = jnp.where(lane_kv == k, rows, 0.0).astype(BF16)

    s_came.wait()
    for j in range(1, 4):
        send(s_all.at[y], s_all.at[y], 28 + j, y_dev(j))

    dstate_wide = jnp.where(same_kv, jnp.concatenate([dstate] * KV_HEADS, axis=1), 0.0).astype(BF16)
    drow[...] = jnp.zeros((16, D), F32)
    for r in range(32):
        drow[0:1, r * 128 : (r + 1) * 128] = dstate[r : r + 1, :]
    spread[32:48, :] = drow[...].astype(BF16)
    for n in range(0, 4):
        cols = slice(n * 512, (n + 1) * 512)
        spread[0:32, cols] = (dot(dstate_wide, wv_in[cols, :], 1, 1) * ga_in[:, cols]).astype(BF16)

    sums = []
    for order in range(2):
        for side in (1, 3):
            for n in (1, 2):
                arrived(ring(order, side, n), ring_sem(order, side, n))
        for part, side in ((low, 1), (high, 3)):
            piece = v1_part(order, 0, part)[...].astype(F32)
            piece = piece + ring(order, side, 2)[...].astype(F32)
            sums.append(piece + ring(order, 4 - side, 1)[...].astype(F32))
    acc_a = jnp.concatenate(sums[0:2], axis=0)
    acc_b = jnp.concatenate(sums[2:4], axis=0)
    v2a[...] = acc_a.astype(BF16)
    v2b[...] = acc_b.astype(BF16)
    for j in range(1, 4):
        send(v2a.at[lax.rem(y + j, 4)], va2.at[j - 1], 56 + j, y_dev(j))
        send(v2b.at[lax.rem(x + j, 4)], vb2.at[j - 1], 60 + j, x_dev(j))

    for n in range(4, 8):
        cols = slice(n * 512, (n + 1) * 512)
        spread[0:32, cols] = (dot(dstate_wide, wv_in[cols, :], 1, 1) * ga_in[:, cols]).astype(BF16)

    for j in range(1, 4):
        arrived(s_all.at[lax.rem(y + 4 - j, 4)], 28 + j)
    for s in range(16):
        block = s_all[:, s].reshape(64, 128)
        rhs_all[s * 128 : s * 128 + 64, 0:128] = block
        rhs_all[s * 128 + 64 : (s + 1) * 128, 128:256] = block
    grads = dot(lhs_all[...], rhs_all[...], 1, 0).astype(BF16)
    for to in range(8):
        xp, xl, cr = to // 4, (to // 2) % 2, to % 2
        for k in range(4):
            first = k * 64 + xl * 32 + cr * 16
            w_send[xp * 2 + xl, cr, :, k * 128 : (k + 1) * 128] = grads[
                first : first + 16, xp * 128 : (xp + 1) * 128
            ]
    for j in range(1, 4):
        send(w_send.at[lax.rem(x + j, 4), core], w_recv.at[x, core], 32 + j, x_dev(j))
        send(w_send.at[lax.rem(x + j, 4), other], w_recv.at[x, core], 36 + j, x_far(j))
    send(w_send.at[x, other], w_recv.at[x, core], 36, sibling)
    keep_w = pltpu.make_async_copy(w_send.at[x, core], w_recv.at[x, core], one_recv.at[32])
    keep_w.start()

    for j in range(1, 4):
        arrived(va2.at[j - 1], 56 + j)
        arrived(vb2.at[j - 1], 60 + j)
    acc_a = v2a[y].astype(F32)
    acc_b = v2b[x].astype(F32)
    for j in range(3):
        acc_a = acc_a + va2[j].astype(F32)
        acc_b = acc_b + vb2[j].astype(F32)
    pieces = [acc_a[:, j * 128 : (j + 1) * 128] for j in range(8)]
    pieces += [acc_b[:, j * 128 : (j + 1) * 128] for j in range(8)]
    stacked = jnp.concatenate([piece.astype(BF16) for piece in pieces], axis=0)
    v3[...] = dot(perm[...], stacked, 1, 0).astype(BF16).reshape(16, 16, 128)
    v3_came = spray(6, grp_dev, lambda j: v3.at[lax.rem(i + j, 16)], lambda j: v3_recv.at[i], v3_recv)

    loss = total(jnp.log(totals) + 50.0 - acc[:, 256:512]) * (1.0 / 256.0)
    loss_out[...] = jnp.broadcast_to(loss, (1, 128))

    mix = dot(spread[0:32, :], h_in[...], 1, 1)
    mean_row = jnp.sum(weights * mix, axis=0, keepdims=True) * (rs_row * rs_row * rs_row) * (1.0 / D)
    mean_all = jnp.transpose(jnp.broadcast_to(mean_row, (128, 256)))


    def hidden_rows(b):
        rows = slice(b * 128, (b + 1) * 128)
        for n in range(8):
            cols = slice(n * 512, (n + 1) * 512)
            grad = dot(wts_t[rows, :], spread[:, cols], 1, 0)
            scale = jnp.concatenate([mean_all[rows]] * 4, axis=1)
            hg[b, :, cols] = (grad - h_in[rows, cols].astype(F32) * scale).astype(BF16)
        copy = pltpu.make_async_copy(hg.at[b], hidden_out.at[pl.ds(b * 128, 128)], out_sem.at[1 + b])
        copy.start()
        return copy

    out_h = [hidden_rows(0), hidden_rows(1)]

    keep_w.wait()
    arrived(w_recv.at[x, other], 36)
    for j in range(1, 4):
        arrived(w_recv.at[lax.rem(x + 4 - j, 4), core], 32 + j)
        arrived(w_recv.at[lax.rem(x + 4 - j, 4), other], 36 + j)
    for h in range(2):
        acc_w = w_recv[0, h].astype(F32)
        for s in range(1, 4):
            acc_w = acc_w + w_recv[s, h].astype(F32)
        wg[:, h * 512 : (h + 1) * 512] = acc_w
    out_w = pltpu.make_async_copy(wg, weight_out, out_sem.at[3])
    out_w.start()

    for copy in sends:
        copy.wait_send()
    for wait in sprays:
        wait.wait()
    out_p.wait()
    for copy in out_h:
        copy.wait()
    out_w.wait()

    v3_came.wait()
    halves = []
    for h in range(2):
        acc_q = v3_recv[h].astype(F32)
        for s in range(1, 8):
            acc_q = acc_q + v3_recv[2 * s + h].astype(F32)
        halves.append(acc_q)
    q_sum = jnp.concatenate(halves, axis=0)
    own = q_rows[...]
    own_square = total(own * own) + 1e-06
    own_dot = total(own * q_sum)
    qg[...] = (q_sum - own * (own_dot / own_square)) * lax.rsqrt(own_square)
    out_q = pltpu.make_async_copy(qg, query_out, out_sem.at[4])
    out_q.start()
    out_q.wait()


def hand_on(
    l_in, q_in, p_in, w_in, h_in, l_out, q_out, p_out, w_out, h_out, l_via, q_via, p_via, w_via, h_via, sem_in, sem_out
):
    steps = [(l_in, l_via, l_out), (q_in, q_via, q_out), (w_in, w_via, w_out), (p_in, p_via, p_out)]
    for n in range(4):
        rows = pl.ds(n * 64, 64)
        steps.append((h_in.at[rows], h_via.at[rows], h_out.at[rows]))
    loads = [pltpu.make_async_copy(src, via, sem_in.at[n]) for n, (src, via, _) in enumerate(steps)]
    stores = [pltpu.make_async_copy(via, dst, sem_out.at[n]) for n, (_, via, dst) in enumerate(steps)]
    for load in loads:
        load.start()
    for load, store in zip(loads, stores):
        load.wait()
        store.start()
    for store in stores:
        store.wait()


def per_device(
    queries, passages, positives, hidden, gain_attn, value_weight, keys, last_query, lengths, gain_final
):
    anywhere = pl.BlockSpec(memory_space=pl.ANY)
    vmem = pltpu.VMEM
    dma = pltpu.SemaphoreType.DMA
    scratch = [
        pltpu.SMEM((1,), jnp.int32), vmem((1, D), BF16), vmem((2, 32, D), BF16), vmem((1, 256), jnp.int32), vmem((SEQ, D), BF16),
        vmem((1, D), F32), vmem((D, KVW), BF16), vmem((SEQ, KVW), BF16), vmem((1, D), BF16),
        vmem((32, 128), F32),
        vmem((256, 256), BF16), vmem((32, 128), F32), vmem((32, 128), F32), vmem((2, 16, 128), BF16),
        vmem((16, 16, 128), BF16), vmem((2, 4, 4, 16, QCOL), BF16), vmem((2, 4, 4, 16, BCOL), BF16), vmem((2, 16, 128), BF16),
        vmem((4, 16, 16, 128), BF16),
        vmem((2, 1, 512), F32), vmem((8, 1, 512), F32), vmem((16, 1, 512), F32), vmem((4, 2, 16, 1024), BF16),
        vmem((4, 2, 16, 1024), BF16), vmem((2, 8, 2, 32, 128), BF16), vmem((16, 2, 32, 128), BF16),
        vmem((256, 2048), BF16), vmem((2048, 256), BF16), vmem((4, 2, 16, 512), BF16), vmem((4, 2, 16, 512), BF16),
        vmem((48, SEQ), BF16), vmem((SEQ, 128), F32), vmem((32, D), F32), vmem((48, D), BF16),
        vmem((16, D), F32), vmem((2, 128, D), BF16),
        vmem((32, D), BF16), vmem((SEQ, 48), BF16),
        vmem((2, 4, 4, 16, QCOL), BF16), vmem((6, 2, 16, QCOL), BF16), vmem((6, 2, 16, QCOL), BF16),
        vmem((4, 2, 16, QCOL), BF16),
        vmem((4, 16, QCOL), BF16), vmem((4, 16, QCOL), BF16), vmem((3, 16, QCOL), BF16),
        vmem((3, 16, QCOL), BF16), vmem((16, 16, 128), BF16), vmem((16, 16, 128), BF16),
        vmem((16, KVW), F32), vmem((32, 128), F32),
        dma((10,)), dma((5,)), dma((7,)), dma((7,)), dma((64,)), dma((64,)), dma((1,)),
    ]
    loss, query_grad, passage_grad, weight_grad, hidden_grad = pl.pallas_call(
        kernel,
        out_shape=(
            jax.ShapeDtypeStruct((1, 128), F32),
            jax.ShapeDtypeStruct((32, 128), F32),
            jax.ShapeDtypeStruct((32, D), F32),
            jax.ShapeDtypeStruct((16, KVW), F32),
            jax.ShapeDtypeStruct((SEQ, D), BF16),
        ),
        in_specs=[anywhere] * 10,
        out_specs=(pl.BlockSpec(memory_space=pltpu.VMEM),) + (anywhere,) * 4,
        scratch_shapes=scratch,
        compiler_params=pltpu.CompilerParams(
            collective_id=0, has_side_effects=True, vmem_limit_bytes=56 * 1024 * 1024
        ),
    )(
        lengths, queries, passages, positives.reshape(1, 256), hidden.reshape(SEQ, D),
        gain_attn.reshape(1, D), value_weight, keys.reshape(SEQ, KVW), last_query,
        gain_final.reshape(32, 128),
    )
    grads = (loss, query_grad, passage_grad, weight_grad, hidden_grad)
    loss, query_grad, passage_grad, weight_grad, hidden_grad = pl.pallas_call(
        hand_on,
        out_shape=tuple(jax.ShapeDtypeStruct(leaf.shape, leaf.dtype) for leaf in grads),
        in_specs=[anywhere] * 5,
        out_specs=(anywhere,) * 5,
        scratch_shapes=[vmem(leaf.shape, leaf.dtype) for leaf in grads] + [dma((8,)), dma((8,))],
        compiler_params=pltpu.CompilerParams(vmem_limit_bytes=56 * 1024 * 1024),
    )(*grads)
    return (loss[0, 0], query_grad.reshape(1, D), passage_grad, weight_grad, hidden_grad.reshape(1, SEQ, D))


def solution(mesh):
    placed = (
        P("dp", None),
        P("dp", None),
        P(),
        P("dp", None, None),
        P(),
        P(),
        P("dp", None, None),
        P("dp", None),
        P("dp"),
        P(),
    )
    return jax.shard_map(
        per_device,
        mesh=mesh,
        in_specs=placed,
        out_specs=(P(), P("dp", None), P("dp", None), P("dp", None), P("dp", None, None)),
        check_vma=False,
    )
```

time: 1800 us -> 65.7 us (0.04)
  waiting for transfers between devices: 1630 us -> 0 us
  blocking collectives: 74.8 us -> 0 us
  Pallas kernels: 0 us -> 64.2 us
  matrix products: 42.3 us -> 0 us
  other arithmetic: 27.7 us -> 0 us
    reduce_scatter x1 -> x0, waiting for transfers between devices: 1290 us -> none  [per_device(): lax.psum_scatter(lax.dot_general(block, dvalues_full, (((0,), (0,)), ((),...]
    unnamed x4 -> x0, waiting for transfers between devices: 233 us -> none
    all_gather x1 -> x0, waiting for transfers between devices: 110 us -> none  [per_device(): every_query = lax.all_gather(queries, 'dp', axis=0, tiled=True)]
    psum x1 -> x0, blocking collectives: 74.8 us -> none  [per_device(): lax.psum((jnp.sum(expo_terms, axis=1), jnp.sum(target * scores, axis=1)),...]
    pallas_call x0 -> x2, Pallas kernels: none -> 64.2 us  [the longest x1 61.4 us: per_device(): pl.pallas_call(kernel, out_shape=(jax.ShapeDtypeStruct((1, 128), F32), ja...]
    dot_general x10 -> x0, matrix products: 42.3 us -> none  [the longest x1 13.1 us: per_device(): lax.dot_general(block, dvalues_full, (((0,), (0,)), ((), ())), precision=...]
  transfers between devices with their start and end apart: 3 -> 0, of which waited for: 3 -> 0; matrix products, arithmetic and copies ran while one was open for 3% -> 0% of each run, Pallas kernels for 0% -> 0%
where the time goes in v1:
time: 65.7 us; the launch traced here: 65.5 us
  Pallas kernels  64.2 us (98%)
  between operations  1.29 us (2%)
    pallas_call x1, Pallas kernels, per_device(): pl.pallas_call(kernel, out_shape=(jax.ShapeDtypeStruct((1, 128), F32), ja...  61.4 us
    pallas_call x1, Pallas kernels, per_device(): pl.pallas_call(hand_on, out_shape=tuple((jax.ShapeDtypeStruct(leaf.shape,...  2.73 us

profile of v1, /device:TPU:1, one launch (start us, length us, event | category | flops | bytes accessed | tf_op | source)
XLA Modules:
  0.0 65.5 jit_solution(14438998340077748473)
XLA Ops:
  1.3 61.4 %shard_map.137 = (f32[1,128]{1,0:T(1,128)}, f32[32,128]{1,0:T(8,128)}, f32[32,4096]{1,0:T(8,128)}, f32[16,1024]{1,0:T(8,128)}, bf16[256,4096]{1,0:T(8,128)(2,1)}) custom-call(s32[1]{0:T(128)S(6)} %copy.15.lengths, bf16[1,4096]{1,0:T(2,128)(2,1)} %queries.1, bf16[32,4096]{1,0:T(8,128)(2,1)} %passages.1, s32[1,256]{1,0:T(1,128)} %bitcast.13, ...), custom_call_target="tpu_custom_call" | custom-call | tf_op jit(solution)/shard_map/pallas_call | solution.py:571
  62.7 2.7 %shard_map.138 = (f32[1,128]{1,0:T(1,128)}, f32[32,128]{1,0:T(8,128)}, f32[32,4096]{1,0:T(8,128)}, f32[16,1024]{1,0:T(8,128)}, bf16[256,4096]{1,0:T(8,128)(2,1)}) custom-call(f32[1,128]{1,0:T(1,128)} %get-tuple-element.15.l_in, f32[32,128]{1,0:T(8,128)} %get-tuple-element.16.q_in, f32[32,4096]{1,0:T(8,128)} %get-tuple-element.17.p_in, ...), custom_call_target="tpu_custom_call" | custom-call | tf_op jit(solution)/shard_map/pallas_call | solution.py:592

commit v2 on v1

--- a/solution.py
+++ b/solution.py
@@ -35,7 +35,7 @@
     len_in, q_in, p_all, pos_in, h_in, ga_in, wv_in, k_in, lq_in, gf_in,
     perm, rows32, q_rows, q_half, q_recv, q_a, q_b, s_own, s_all,
     tot_own, tot_a, tot_b, pool_own, pool_recv, pool_t, pool_rows, lhs_all, rhs_all, w_send, w_recv,
-    wts, hcol, pg, spread, drow, hg, pool_rows32, wts_t,
+    wts, hcol, pg, spread, drow, hg, pool_rows32, wts_t, g_own, d_sib,
     v1, va1, vb1, v_fwd, v2a, v2b, va2, vb2, v3, v3_recv, wg, qg,
     in_sem, out_sem, grp_send, grp_recv, one_send, one_recv, loc_sem,
 ):
@@ -52,40 +52,49 @@
         return g * 16 + lax.rem(i + 2 * j, 16)
 
     def xy_dev(j):
-        return lax.rem(g + j, 16) * 16 + i
+        return (lax.rem(x + j // 4, 4) * 4 + lax.rem(y + j % 4, 4)) * 16 + i
 
     def x_dev(j):
         return (lax.rem(x + j, 4) * 4 + y) * 16 + i
 
     def y_dev(j):
         return (x * 4 + lax.rem(y + j, 4)) * 16 + i
+
+    def outward(k, mid):
+        return mid + ((k + 1) // 2) * (1 - 2 * (k % 2))
+
+    def outward_xy(k):
+        return outward(k // 4, 2) * 4 + outward(k % 4, 2)
+
+    l_query = pltpu.make_async_copy(queries, q_in, in_sem.at[0])
+    l_query.start()
+
+    barrier = pltpu.get_barrier_semaphore()
+
+    def greet(k, _):
+        pl.semaphore_signal(barrier, inc=1, device_id=(grp_dev(outward(k, 8)),), device_id_type=MESH)
+        pl.semaphore_signal(barrier, inc=1, device_id=(xy_dev(outward_xy(k)),), device_id_type=MESH)
+        return 0
+
+    lax.fori_loop(0, 15, greet, 0, unroll=True)
+
+    def x_far(j):
+        return x_dev(j) + 1 - 2 * core
+
+    for j in range(1, 4):
+        pl.semaphore_signal(barrier, inc=1, device_id=(x_far(j),), device_id_type=MESH)
 
     loads = []
     for n, (src, dst) in enumerate(
         (
-            (queries, q_in), (lengths, len_in), (last_query, lq_in), (keys, k_in), (passages, p_all.at[core]), (hidden, h_in),
+            (lengths, len_in), (last_query, lq_in), (keys, k_in), (passages, p_all.at[core]), (hidden, h_in),
             (value_weight, wv_in), (positives, pos_in), (gain_attn, ga_in), (gain_final, gf_in),
         )
     ):
-        copy = pltpu.make_async_copy(src, dst, in_sem.at[n])
+        copy = pltpu.make_async_copy(src, dst, in_sem.at[n + 1])
         copy.start()
         loads.append(copy)
-    l_query, l_len, l_last, l_keys, l_pass, l_hidden, l_value, l_pos, l_ga, l_gf = loads
-
-    barrier = pltpu.get_barrier_semaphore()
-
-    def greet(j, _):
-        pl.semaphore_signal(barrier, inc=1, device_id=(grp_dev(j),), device_id_type=MESH)
-        pl.semaphore_signal(barrier, inc=1, device_id=(xy_dev(j),), device_id_type=MESH)
-        return 0
-
-    lax.fori_loop(1, 16, greet, 0, unroll=True)
-
-    def x_far(j):
-        return x_dev(j) + 1 - 2 * core
-
-    for j in range(1, 4):
-        pl.semaphore_signal(barrier, inc=1, device_id=(x_far(j),), device_id_type=MESH)
+    l_len, l_last, l_keys, l_pass, l_hidden, l_value, l_pos, l_ga, l_gf = loads
 
     sends = []
 
@@ -106,14 +115,15 @@
     sprays = []
 
     def spray(n, device, src_of, dst_of, whole, stop=16):
-        def step(j, _):
+        def step(k, _):
+            j = outward_xy(k) if device is xy_dev else outward(k, stop // 2)
             pltpu.make_async_remote_copy(
                 src_ref=src_of(j), dst_ref=dst_of(j), send_sem=grp_send.at[n], recv_sem=grp_recv.at[n],
                 device_id=(device(j),), device_id_type=MESH,
             ).start()
             return 0
 
-        lax.fori_loop(1, stop, step, 0, unroll=True)
+        lax.fori_loop(0, stop - 1, step, 0, unroll=True)
         pltpu.make_async_copy(src_of(0), dst_of(0), grp_recv.at[n]).start()
         some = whole.at[pl.ds(0, stop - 1)]
         sprays.append(pltpu.make_async_copy(some, some, grp_send.at[n]))
@@ -166,14 +176,6 @@
             q_a[core, x, y, :, j * 128 : (j + 1) * 128] = part
         else:
             q_b[core, x, y, :, (j - 8) * 128 : (j - 7) * 128] = part
-    square = jnp.broadcast_to(jnp.sum(square, axis=1, keepdims=True), (16, 128))
-    top = square.astype(BF16)
-    mid = (square - top.astype(F32)).astype(BF16)
-    low = square - top.astype(F32) - mid.astype(F32)
-    lane = lax.broadcasted_iota(jnp.int32, (16, 128), 1)
-    ext = jnp.where(lane == 0, top.astype(F32), jnp.where(lane == 1, mid.astype(F32), jnp.where(lane == 2, low, 0.0)))
-    q_b[core, x, y, :, QCOL:BCOL] = ext.astype(BF16)
-
     low, high, every = pl.ds(0, 2), pl.ds(2, 2), slice(None)
 
     def rest_of(order, h, near, part=every):
@@ -188,10 +190,6 @@
     def pass_ref(ref, n, dev):
         send(ref, ref, n, dev)
 
-    def q_block():
-        for j in range(1, 4):
-            pass_ref(q_a.at[core, x, y], j, y_dev(j))
-            pass_ref(q_b.at[core, x, y], 4 + j, x_dev(j))
 
     def q_line():
         for j in range(1, 4):
@@ -211,6 +209,7 @@
                 arrived(rest_of(order, core, near), 8 + 4 * order + side)
                 pass_ref(rest_of(order, core, near, part), 8 + 4 * order + (2 if side == 1 else 0), along(order, side))
                 pass_ref(rest_of(order, core, near), 16 + 4 * order + side, sibling)
+    def q_rest():
         for side, part in ((1, low), (3, high)):
             for order in range(2):
                 far = lax.rem(here(order) + 2, 4)
@@ -228,7 +227,17 @@
     def q_block_of(h, order):
         return (q_b if order else q_a)[h, :, :, :, 0:QCOL].reshape(256, QCOL)
 
-    q_block()
+    for j in range(1, 4):
+        pass_ref(q_a.at[core, x, y], j, y_dev(j))
+    square = jnp.broadcast_to(jnp.sum(square, axis=1, keepdims=True), (16, 128))
+    top = square.astype(BF16)
+    mid = (square - top.astype(F32)).astype(BF16)
+    bottom = square - top.astype(F32) - mid.astype(F32)
+    lane = lax.broadcasted_iota(jnp.int32, (16, 128), 1)
+    ext = jnp.where(lane == 0, top.astype(F32), jnp.where(lane == 1, mid.astype(F32), jnp.where(lane == 2, bottom, 0.0)))
+    q_b[core, x, y, :, QCOL:BCOL] = ext.astype(BF16)
+    for j in range(1, 4):
+        pass_ref(q_b.at[core, x, y], 4 + j, x_dev(j))
 
     l_hidden.wait()
 
@@ -280,20 +289,29 @@
     keep_pool = pltpu.make_async_copy(pool_own.at[y], pool_recv.at[y], one_recv.at[24])
     keep_pool.start()
 
-    rhs_all[...] = jnp.zeros((2048, 256), BF16)
-
-    q_finish()
+    final = final + context(1)
+    for r in range(32):
+        rows32[r : r + 1, :] = drow[0:1, r * 128 : (r + 1) * 128]
+    final = final + rows32[...]
+    oscale = lax.rsqrt(total(final * final) * (1.0 / D) + 1e-05)
+
+    q_rest()
+
     l_pos.wait()
     three = jnp.where(lax.broadcasted_iota(jnp.int32, (16, 128), 1) < 3, 1.0, 0.0).astype(BF16)
-    dots = jnp.zeros((64, 256), F32)
-    q_square = jnp.zeros((16, 256), F32)
-    for h in range(2):
+
+    def half_scores(h):
+        rows = jnp.zeros((64, 256), F32)
         for order in range(2):
-            first = h * HALF + order * QCOL
-            dots = dots + dot(
-                p_all[:, :, first : first + QCOL].reshape(64, QCOL), q_block_of(h, order), 1, 1
-            )
-        q_square = q_square + dot(three, q_b[h, :, :, :, QCOL:BCOL].reshape(256, 128), 1, 1)
+            cols = pl.ds(pl.multiple_of(h * HALF + order * QCOL, QCOL), QCOL)
+            rows = rows + dot(p_all[:, :, cols].reshape(64, QCOL), q_block_of(h, order), 1, 1)
+        return rows, dot(three, q_b[h, :, :, :, QCOL:BCOL].reshape(256, 128), 1, 1)
+
+    dots_here, square_here = half_scores(core)
+    q_finish()
+    dots_there, square_there = half_scores(other)
+    dots = dots_here + dots_there
+    q_square = square_here + square_there
     q_norm = jnp.sqrt(q_square[0:1, :] + 1e-06)
     cosine = dots / (p_norm * q_norm)
     scores = 50.0 * cosine
@@ -317,6 +335,8 @@
         lambda j: pool_t.at[lax.rem(i + j, 2), lax.rem(i + j, 16) // 2], lambda j: pool_rows.at[i], pool_rows,
     )
 
+    rhs_all[...] = jnp.zeros((2048, 256), BF16)
+
     tot_came.wait()
     acc = tot_a[0]
     for s in range(1, 8):
@@ -324,11 +344,6 @@
     tot_own[1] = acc
     tot_came = spray(4, xy_dev, lambda j: tot_own.at[1], lambda j: tot_b.at[g], tot_b)
 
-    final = final + context(1)
-    for r in range(32):
-        rows32[r : r + 1, :] = drow[0:1, r * 128 : (r + 1) * 128]
-    final = final + rows32[...]
-    oscale = lax.rsqrt(total(final * final) * (1.0 / D) + 1e-05)
     inv_p = 1.0 / p_norm
     tot_came.wait()
     acc = tot_b[0]
@@ -370,6 +385,30 @@
     out_p = pltpu.make_async_copy(pg, passage_out, out_sem.at[0])
     out_p.start()
 
+    def ring_on(order):
+        for side, part in ((1, low), (3, high)):
+            arrived(ring(order, side, 0), ring_sem(order, side, 0))
+            added = v1_part(order, side, part)[...].astype(F32) + ring(order, side, 0)[...].astype(F32)
+            slot = order * 2 + (0 if side == 1 else 1)
+            v_fwd[slot] = added.astype(BF16)
+            send(v_fwd.at[slot], ring(order, side, 2), ring_sem(order, side, 2), along(order, side))
+
+    def ring_end(order):
+        second = v2b if order else v2a
+        for side in (1, 3):
+            for n in (1, 2):
+                arrived(ring(order, side, n), ring_sem(order, side, n))
+        for part, side in ((low, 1), (high, 3)):
+            piece = v1_part(order, 0, part)[...].astype(F32)
+            piece = piece + ring(order, side, 2)[...].astype(F32)
+            piece = piece + ring(order, 4 - side, 1)[...].astype(F32)
+            second[part] = piece.astype(BF16)
+        for j in range(1, 4):
+            if order == 0:
+                send(v2a.at[lax.rem(y + j, 4)], va2.at[j - 1], 56 + j, y_dev(j))
+            else:
+                send(v2b.at[lax.rem(x + j, 4)], vb2.at[j - 1], 60 + j, x_dev(j))
+
     for r in range(32):
         rows32[r : r + 1, :] = pg[0:1, r * 128 : (r + 1) * 128]
     l_gf.wait()
@@ -378,15 +417,39 @@
     dstate = oscale * (upstream - final * (oscale * oscale) * mean_uf)
     s_own[0] = dstate[0:16, :].astype(BF16)
     s_own[1] = dstate[16:32, :].astype(BF16)
+    send(s_own.at[other], d_sib, 28, sibling)
     s_came = spray(5, grp_dev, lambda j: s_own.at[lax.rem(i + j, 2)], lambda j: s_all.at[y, i], s_all.at[y])
 
-    for order in range(2):
-        for side, part in ((1, low), (3, high)):
-            arrived(ring(order, side, 0), ring_sem(order, side, 0))
-            added = v1_part(order, side, part)[...].astype(F32) + ring(order, side, 0)[...].astype(F32)
-            slot = order * 2 + (0 if side == 1 else 1)
-            v_fwd[slot] = added.astype(BF16)
-            send(v_fwd.at[slot], ring(order, side, 2), ring_sem(order, side, 2), along(order, side))
+    ring_on(0)
+    ring_on(1)
+
+    arrived(d_sib, 28)
+    head16 = (lax.broadcasted_iota(jnp.int32, (32, 512), 0) & 15) >> 2
+    kv16 = lax.broadcasted_iota(jnp.int32, (32, 512), 1) >> 7
+    both_d = jnp.concatenate([jnp.where(core == 0, dstate[0:16], dstate[16:32]), d_sib[...].astype(F32)], axis=0)
+    both_d = jnp.where(head16 == kv16, jnp.concatenate([both_d] * 4, axis=1), 0.0).astype(BF16)
+    my_kv = pl.ds(pl.multiple_of(core * 512, 512), 512)
+
+    def spread_piece(n):
+        cols = slice(n * 512, (n + 1) * 512)
+        piece = (dot(both_d, wv_in[cols, my_kv], 1, 1) * ga_in[:, cols]).astype(BF16)
+        spread[core, :, cols] = piece[0:16, :]
+        g_own[n // 4, :, (n % 4) * 512 : (n % 4 + 1) * 512] = piece[16:32, :]
+        if n % 4 == 3:
+            dst = spread.at[core, :, pl.ds((n // 4) * HALF, HALF)]
+            send(g_own.at[n // 4], dst, 48 + 8 * (n // 4), sibling)
+
+    for n in range(0, 4):
+        spread_piece(n)
+    ring_end(0)
+    ring_end(1)
+
+    s_came.wait()
+    for j in range(1, 4):
+        send(s_all.at[y], s_all.at[y], 28 + j, y_dev(j))
+
+    for n in range(4, 8):
+        spread_piece(n)
 
     rows_came.wait()
     lane_kv = (lax.broadcasted_iota(jnp.int32, (64, 128), 1) & 15) >> 2
@@ -395,39 +458,19 @@
         for k in range(4):
             lhs_all[k * 64 : (k + 1) * 64, s * 128 : (s + 1) * 128] = jnp.where(lane_kv == k, rows, 0.0).astype(BF16)
 
-    s_came.wait()
-    for j in range(1, 4):
-        send(s_all.at[y], s_all.at[y], 28 + j, y_dev(j))
-
-    dstate_wide = jnp.where(same_kv, jnp.concatenate([dstate] * KV_HEADS, axis=1), 0.0).astype(BF16)
-    drow[...] = jnp.zeros((16, D), F32)
-    for r in range(32):
-        drow[0:1, r * 128 : (r + 1) * 128] = dstate[r : r + 1, :]
-    spread[32:48, :] = drow[...].astype(BF16)
-    for n in range(0, 4):
-        cols = slice(n * 512, (n + 1) * 512)
-        spread[0:32, cols] = (dot(dstate_wide, wv_in[cols, :], 1, 1) * ga_in[:, cols]).astype(BF16)
-
-    sums = []
-    for order in range(2):
-        for side in (1, 3):
-            for n in (1, 2):
-                arrived(ring(order, side, n), ring_sem(order, side, n))
-        for part, side in ((low, 1), (high, 3)):
-            piece = v1_part(order, 0, part)[...].astype(F32)
-            piece = piece + ring(order, side, 2)[...].astype(F32)
-            sums.append(piece + ring(order, 4 - side, 1)[...].astype(F32))
-    acc_a = jnp.concatenate(sums[0:2], axis=0)
-    acc_b = jnp.concatenate(sums[2:4], axis=0)
-    v2a[...] = acc_a.astype(BF16)
-    v2b[...] = acc_b.astype(BF16)
-    for j in range(1, 4):
-        send(v2a.at[lax.rem(y + j, 4)], va2.at[j - 1], 56 + j, y_dev(j))
-        send(v2b.at[lax.rem(x + j, 4)], vb2.at[j - 1], 60 + j, x_dev(j))
-
-    for n in range(4, 8):
-        cols = slice(n * 512, (n + 1) * 512)
-        spread[0:32, cols] = (dot(dstate_wide, wv_in[cols, :], 1, 1) * ga_in[:, cols]).astype(BF16)
+    for j in range(1, 4):
+        arrived(va2.at[j - 1], 56 + j)
+        arrived(vb2.at[j - 1], 60 + j)
+    acc_a = v2a[y].astype(F32)
+    acc_b = v2b[x].astype(F32)
+    for j in range(3):
+        acc_a = acc_a + va2[j].astype(F32)
+        acc_b = acc_b + vb2[j].astype(F32)
+    pieces = [acc_a[:, j * 128 : (j + 1) * 128] for j in range(8)]
+    pieces += [acc_b[:, j * 128 : (j + 1) * 128] for j in range(8)]
+    stacked = jnp.concatenate([piece.astype(BF16) for piece in pieces], axis=0)
+    v3[...] = dot(perm[...], stacked, 1, 0).astype(BF16).reshape(16, 16, 128)
+    v3_came = spray(6, grp_dev, lambda j: v3.at[lax.rem(i + j, 16)], lambda j: v3_recv.at[i], v3_recv)
 
     for j in range(1, 4):
         arrived(s_all.at[lax.rem(y + 4 - j, 4)], 28 + j)
@@ -450,33 +493,24 @@
     keep_w = pltpu.make_async_copy(w_send.at[x, core], w_recv.at[x, core], one_recv.at[32])
     keep_w.start()
 
-    for j in range(1, 4):
-        arrived(va2.at[j - 1], 56 + j)
-        arrived(vb2.at[j - 1], 60 + j)
-    acc_a = v2a[y].astype(F32)
-    acc_b = v2b[x].astype(F32)
-    for j in range(3):
-        acc_a = acc_a + va2[j].astype(F32)
-        acc_b = acc_b + vb2[j].astype(F32)
-    pieces = [acc_a[:, j * 128 : (j + 1) * 128] for j in range(8)]
-    pieces += [acc_b[:, j * 128 : (j + 1) * 128] for j in range(8)]
-    stacked = jnp.concatenate([piece.astype(BF16) for piece in pieces], axis=0)
-    v3[...] = dot(perm[...], stacked, 1, 0).astype(BF16).reshape(16, 16, 128)
-    v3_came = spray(6, grp_dev, lambda j: v3.at[lax.rem(i + j, 16)], lambda j: v3_recv.at[i], v3_recv)
+    drow[...] = jnp.zeros((16, D), F32)
+    for r in range(32):
+        drow[0:1, r * 128 : (r + 1) * 128] = dstate[r : r + 1, :]
+    spread[2] = drow[...].astype(BF16)
+    for n in range(2):
+        arrived(spread.at[other, :, pl.ds(n * HALF, HALF)], 48 + 8 * n)
+    mix = dot(spread[0:2].reshape(32, D), h_in[...], 1, 1)
+    mean_row = jnp.sum(weights * mix, axis=0, keepdims=True) * (rs_row * rs_row * rs_row) * (1.0 / D)
+    mean_all = jnp.transpose(jnp.broadcast_to(mean_row, (128, 256)))
 
     loss = total(jnp.log(totals) + 50.0 - acc[:, 256:512]) * (1.0 / 256.0)
     loss_out[...] = jnp.broadcast_to(loss, (1, 128))
-
-    mix = dot(spread[0:32, :], h_in[...], 1, 1)
-    mean_row = jnp.sum(weights * mix, axis=0, keepdims=True) * (rs_row * rs_row * rs_row) * (1.0 / D)
-    mean_all = jnp.transpose(jnp.broadcast_to(mean_row, (128, 256)))
-
 
     def hidden_rows(b):
         rows = slice(b * 128, (b + 1) * 128)
         for n in range(8):
             cols = slice(n * 512, (n + 1) * 512)
-            grad = dot(wts_t[rows, :], spread[:, cols], 1, 0)
+            grad = dot(wts_t[rows, :], spread[:, :, cols].reshape(48, 512), 1, 0)
             scale = jnp.concatenate([mean_all[rows]] * 4, axis=1)
             hg[b, :, cols] = (grad - h_in[rows, cols].astype(F32) * scale).astype(BF16)
         copy = pltpu.make_async_copy(hg.at[b], hidden_out.at[pl.ds(b * 128, 128)], out_sem.at[1 + b])
@@ -502,11 +536,6 @@
         copy.wait_send()
     for wait in sprays:
         wait.wait()
-    out_p.wait()
-    for copy in out_h:
-        copy.wait()
-    out_w.wait()
-
     v3_came.wait()
     halves = []
     for h in range(2):
@@ -521,6 +550,10 @@
     qg[...] = (q_sum - own * (own_dot / own_square)) * lax.rsqrt(own_square)
     out_q = pltpu.make_async_copy(qg, query_out, out_sem.at[4])
     out_q.start()
+    out_p.wait()
+    for copy in out_h:
+        copy.wait()
+    out_w.wait()
     out_q.wait()
 
 
@@ -558,9 +591,9 @@
         vmem((2, 1, 512), F32), vmem((8, 1, 512), F32), vmem((16, 1, 512), F32), vmem((4, 2, 16, 1024), BF16),
         vmem((4, 2, 16, 1024), BF16), vmem((2, 8, 2, 32, 128), BF16), vmem((16, 2, 32, 128), BF16),
         vmem((256, 2048), BF16), vmem((2048, 256), BF16), vmem((4, 2, 16, 512), BF16), vmem((4, 2, 16, 512), BF16),
-        vmem((48, SEQ), BF16), vmem((SEQ, 128), F32), vmem((32, D), F32), vmem((48, D), BF16),
+        vmem((48, SEQ), BF16), vmem((SEQ, 128), F32), vmem((32, D), F32), vmem((3, 16, D), BF16),
         vmem((16, D), F32), vmem((2, 128, D), BF16),
-        vmem((32, D), BF16), vmem((SEQ, 48), BF16),
+        vmem((32, D), BF16), vmem((SEQ, 48), BF16), vmem((2, 16, HALF), BF16), vmem((16, 128), BF16),
         vmem((2, 4, 4, 16, QCOL), BF16), vmem((6, 2, 16, QCOL), BF16), vmem((6, 2, 16, QCOL), BF16),
         vmem((4, 2, 16, QCOL), BF16),
         vmem((4, 16, QCOL), BF16), vmem((4, 16, QCOL), BF16), vmem((3, 16, QCOL), BF16),

time: 65.7 us -> 65.6 us (level)
  no operation moved by 1% of the time
where the time goes in v2:
time: 65.6 us; the launch traced here: 65.4 us
  Pallas kernels  64.2 us (98%)
  between operations  1.29 us (2%)
    pallas_call x1, Pallas kernels, per_device(): pl.pallas_call(kernel, out_shape=(jax.ShapeDtypeStruct((1, 128), F32), ja...  61.4 us
    pallas_call x1, Pallas kernels, per_device(): pl.pallas_call(hand_on, out_shape=tuple((jax.ShapeDtypeStruct(leaf.shape,...  2.73 us

profile of v2, /device:TPU:1, one launch (start us, length us, event | category | flops | bytes accessed | tf_op | source)
XLA Modules:
  0.0 65.4 jit_solution(12412530836879980825)
XLA Ops:
  1.3 61.4 %shard_map.137 = (f32[1,128]{1,0:T(1,128)}, f32[32,128]{1,0:T(8,128)}, f32[32,4096]{1,0:T(8,128)}, f32[16,1024]{1,0:T(8,128)}, bf16[256,4096]{1,0:T(8,128)(2,1)}) custom-call(s32[1]{0:T(128)S(6)} %copy.15.lengths, bf16[1,4096]{1,0:T(2,128)(2,1)} %queries.1, bf16[32,4096]{1,0:T(8,128)(2,1)} %passages.1, s32[1,256]{1,0:T(1,128)} %bitcast.13, ...), custom_call_target="tpu_custom_call" | custom-call | tf_op jit(solution)/shard_map/pallas_call | solution.py:604
  62.7 2.7 %shard_map.138 = (f32[1,128]{1,0:T(1,128)}, f32[32,128]{1,0:T(8,128)}, f32[32,4096]{1,0:T(8,128)}, f32[16,1024]{1,0:T(8,128)}, bf16[256,4096]{1,0:T(8,128)(2,1)}) custom-call(f32[1,128]{1,0:T(1,128)} %get-tuple-element.15.l_in, f32[32,128]{1,0:T(8,128)} %get-tuple-element.16.q_in, f32[32,4096]{1,0:T(8,128)} %get-tuple-element.17.p_in, ...), custom_call_target="tpu_custom_call" | custom-call | tf_op jit(solution)/shard_map/pallas_call | solution.py:625
